TPU v7x, 32 devices: a whole 2x2x4 slice. The times are simulated.
32 devices in a mesh: groups: 2 (over y), loop: 4 (over z), enc: 2 (over x), rep: 2 (over core).
Axes of the slice: x: 2, y: 2, z: 4, core: 2. Of those that a mesh axis runs over, the one named last changes fastest.
Arguments:
- embeddings: bfloat16 [4096, 768], P(('groups', 'loop', 'rep'), 'enc'), parts along dimension 0, may hold values from -24 to 24
- head_weight: bfloat16 [768, 768], P('enc'), may hold values from -0.21875 to 0.21875
- gp_weights: float32 [4096], P('groups'), parts along dimension 0, may hold values from -24 to 24
- counts: int32 [8], P('groups'), parts along dimension 0, may hold values from 64 to 512, as said below
Outputs:
- embed_grad: bfloat16 [4096, 768], P(('groups', 'loop', 'rep'), 'enc'), parts along dimension 0
- head_grad: float32 [1536, 768], P(('groups', 'enc')), parts along dimension 0
There are 2 independent parts, one for each index of `groups`. A program takes and returns all parts, laid end to end along the dimension named above; an argument that names none is the same for every part. Nothing has to cross between parts.
Inputs may be any that keep to these rules, and one draw needn't show every extreme that they name: `counts`: some block is full and some block holds exactly 64 valid molecules.
All inputs are finite; a program needn't handle non-finite values.
Results may differ from a plain program's by a relative error of at most 0.019.
Values may be sent and summed in bfloat16 or wider, within the bound.
A program may use at most 64 MiB of HBM per device.

v0:
```python
import jax
import jax.numpy as jnp
from jax import lax
from jax.sharding import PartitionSpec as P

EPSILON = 1e-06


def passed_along(value, axis, steps):
    count = lax.axis_size(axis)
    pairs = [(source, (source + steps) % count) for source in range(count)]
    return lax.ppermute(value, axis, pairs)


def pass_forward(piece):
    return passed_along(piece, "loop", 1)


def body(embeddings, head_weight, gp_weights, counts):
    enc_size = lax.axis_size("enc")
    rep_size = lax.axis_size("rep")
    loop_size = lax.axis_size("loop")
    share_rows = embeddings.shape[0]
    piece_rows = share_rows // enc_size
    block_rows = share_rows * rep_size
    loop_index = lax.axis_index("loop")
    enc_index = lax.axis_index("enc")
    rep_index = lax.axis_index("rep")
    rows = embeddings
    own_feats = lax.psum_scatter(
        jnp.dot(rows, head_weight, preferred_element_type=jnp.float32),
        "enc",
        scatter_dimension=0,
        tiled=True,
    ).astype(jnp.bfloat16)
    block_feats = lax.all_gather(own_feats, ("enc", "rep"), axis=0, tiled=True)
    block_norms = jnp.sum(jnp.square(block_feats.astype(jnp.float32)), axis=1)
    offsets = (
        jnp.arange(rep_size, dtype=jnp.int32)[None, :, None] * share_rows
        + jnp.arange(enc_size, dtype=jnp.int32)[:, None, None] * piece_rows
        + jnp.arange(piece_rows, dtype=jnp.int32)[None, None, :]
    ).reshape(block_rows)
    own_base = lax.dynamic_slice_in_dim(gp_weights, loop_index * block_rows, block_rows)
    block_coef = (
        own_base.reshape(rep_size, enc_size, piece_rows).transpose(1, 0, 2).reshape(block_rows)
    )
    own_count = lax.dynamic_index_in_dim(counts, loop_index, keepdims=False)
    block_coef = jnp.where(offsets < own_count, block_coef, 0.0)
    piece_start = rep_index * share_rows + enc_index * piece_rows
    piece_offsets = piece_start + jnp.arange(piece_rows, dtype=jnp.int32)

    def tile(state, piece, anchor):
        anchor_count = lax.dynamic_index_in_dim(counts, anchor, keepdims=False)
        accum, quotient_sum = state
        piece_coef = lax.dynamic_slice_in_dim(
            gp_weights, anchor * block_rows + piece_start, piece_rows
        )
        piece_coef = jnp.where(piece_offsets < anchor_count, piece_coef, 0.0)
        piece_norms = jnp.sum(jnp.square(piece.astype(jnp.float32)), axis=1)
        scores = lax.dot_general(
            piece, block_feats, (((1,), (1,)), ((), ())), preferred_element_type=jnp.float32
        )
        denom = piece_norms[:, None] + block_norms[None, :] - scores + EPSILON
        inverse = 1.0 / (denom * denom)
        pair_coef = piece_coef[:, None] * block_coef[None, :]
        pair_weight = (pair_coef * (piece_norms[:, None] + block_norms[None, :]) * inverse).astype(
            jnp.bfloat16
        )
        quotient_sum = quotient_sum + jnp.sum(pair_coef * 2.0 * scores * inverse, axis=0)
        accum = accum + lax.dot_general(
            pair_weight, piece, (((0,), (0,)), ((), ())), preferred_element_type=jnp.float32
        )
        return (accum, quotient_sum)

    start_state = (
        jnp.zeros((block_rows, block_feats.shape[1]), jnp.float32),
        jnp.zeros((block_rows,), jnp.float32),
    )
    state = tile(start_state, own_feats, loop_index)

    def forward_step(step_index, carry):
        moving, inner = carry
        moving = pass_forward(moving)
        inner = tile(inner, moving, (loop_index - step_index - 1 + loop_size) % loop_size)
        return (moving, inner)

    moving, state = lax.fori_loop(0, loop_size - 1, forward_step, (own_feats, state))
    accum, quotient_sum = state
    grad_block = accum - block_feats.astype(jnp.float32) * quotient_sum[:, None]
    own_grad = lax.psum_scatter(
        grad_block.astype(jnp.bfloat16), ("enc", "rep"), scatter_dimension=0, tiled=True
    )
    piece = lax.all_gather(own_grad, "enc", axis=0, tiled=True)
    back = lax.dot_general(
        piece, head_weight, (((1,), (1,)), ((), ())), preferred_element_type=jnp.float32
    )
    embed_part = back
    rows = embeddings
    head_part = lax.dot_general(
        rows, piece, (((0,), (0,)), ((), ())), preferred_element_type=jnp.float32
    )
    embed_part, head_part = (embed_part, head_part)
    head_grad = lax.psum(head_part, ("loop", "rep"))
    return (embed_part.astype(jnp.bfloat16), head_grad)


def solution(mesh):
    placed = (P(("groups", "loop", "rep"), "enc"), P("enc", None), P("groups"), P("groups"))
    return jax.shard_map(
        body,
        mesh=mesh,
        in_specs=placed,
        out_specs=(P(("groups", "loop", "rep"), "enc"), P(("groups", "enc"), None)),
        check_vma=False,
    )
```

profile of v0, /device:TPU:0, one launch (start us, length us, event | category | flops | bytes accessed | tf_op | source)
XLA Modules:
  0.0 170.0 jit_solution(11172648524668776611)
XLA Ops:
  7.2 1.0 copy-done
  8.2 2.2 %fusion.40 = f32[256,768]{1,0:T(8,128)} fusion(bf16[256,384]{1,0:T(8,128)(2,1)} %param.6, bf16[384,768]{1,0:T(8,128)(2,1)S(1)} %copy-done), kind=kOutput, calls=%fused_computation.56 | convolution fusion | flops 150994944 | bytes 1572864 | tf_op jit(solution)/shard_map/dot_general | solution.py:31
  10.5 0.7 dynamic_slice.37
  11.2 0.8 dynamic_slice.39
  12.0 0.8 compare_select_fusion.1
  12.8 1.5 compare_select_fusion.2
  14.2 16.8 %reduce-scatter.3.cloned.1.call-done = f32[128,768]{1,0:T(8,128)} async-done(((f32[256,768]{1,0:T(8,128)}), f32[128,768]{1,0:T(8,128)}) %reduce-scatter.3.cloned.1.call-update) | async-done | bytes 393232 | tf_op jit(solution)/shard_map/reduce_scatter | solution.py:30
  31.0 1.1 multiply_reduce_fusion.1
  32.1 8.2 %all_gather.6 = bf16[512,768]{1,0:T(8,128)(2,1)S(1)} all-gather(bf16[128,768]{1,0:T(8,128)(2,1)S(1)} %get-tuple-element.541), channel_id=1, replica_groups=mesh['groups'=2,'loop'=4,'enc'=2,'rep'=2] {'enc','rep'}, dimensions={0}, use_global_device_ids=true | all-gather | bytes 983040 | tf_op jit(solution)/shard_map/all_gather | solution.py:36
  41.0 0.5 fusion.30
  41.5 28.3 %while.23 = (s32[]{:T(128)}, bf16[128,768]{1,0:T(8,128)(2,1)S(1)}, f32[512,768]{1,0:T(8,128)S(1)}, f32[512]{0:T(512)S(1)}, s32[]{:T(128)}, /*index=5*/s32[4]{0:T...) while((s32[]{:T(128)}, bf16[128,768]{1,0:T(8,128)(2,1)S(1)}, ...), condition=%wide.region_7.8_spmd.clone.clone, body=%wide.region_4.7_spmd.clone.clone.sunk | while | flops 203260192 | bytes 6246334 | solution.py:87
  41.5 1.5 collective-permute-start
  43.1 0.6 dynamic_slice.49
  43.6 1.4 compare_select_fusion.4
  45.1 5.5 %collective-permute-done = bf16[128,768]{1,0:T(8,128)(2,1)S(1)} collective-permute-done((bf16[128,768]{1,0:T(8,128)(2,1)S(1)}, bf16[128,768]{1,0:T(8,128)(2,1)S(1)}, u32[]{:S(2)}, u32[]{:S(2)}) %collective-permute-start) | collective-permute-done | bytes 196640 | tf_op jit(solution)/shard_map/while/body/eval_jaxpr/ppermute | solution.py:12
  50.6 0.4 fusion.62
  51.1 0.6 convolution_add_fusion.2
  51.8 0.6 dynamic_slice.49
  52.4 1.4 compare_select_fusion.4
  53.8 6.1 %collective-permute-done = bf16[128,768]{1,0:T(8,128)(2,1)S(1)} collective-permute-done((bf16[128,768]{1,0:T(8,128)(2,1)S(1)}, bf16[128,768]{1,0:T(8,128)(2,1)S(1)}, u32[]{:S(2)}, u32[]{:S(2)}) %collective-permute-start) | collective-permute-done | bytes 196640 | tf_op jit(solution)/shard_map/while/body/eval_jaxpr/ppermute | solution.py:12
  60.5 0.6 convolution_add_fusion.2
  61.2 0.6 dynamic_slice.49
  61.8 1.4 compare_select_fusion.4
  63.2 5.4 %collective-permute-done = bf16[128,768]{1,0:T(8,128)(2,1)S(1)} collective-permute-done((bf16[128,768]{1,0:T(8,128)(2,1)S(1)}, bf16[128,768]{1,0:T(8,128)(2,1)S(1)}, u32[]{:S(2)}, u32[]{:S(2)}) %collective-permute-start) | collective-permute-done | bytes 196640 | tf_op jit(solution)/shard_map/while/body/eval_jaxpr/ppermute | solution.py:12
  69.2 0.6 convolution_add_fusion.2
  69.8 1.1 fusion.21
  71.1 20.9 %reduce-scatter.5.cloned.1.call-done = bf16[128,768]{1,0:T(8,128)(2,1)} async-done(((bf16[512,768]{1,0:T(8,128)(2,1)}), bf16[128,768]{1,0:T(8,128)(2,1)}) %reduce-scatter.5.cloned.1.call-update) | async-done | bytes 196624 | tf_op jit(solution)/shard_map/reduce_scatter | solution.py:90
  92.0 7.5 %all_gather.7 = bf16[256,768]{1,0:T(8,128)(2,1)S(1)} all-gather(bf16[128,768]{1,0:T(8,128)(2,1)} %reduce-scatter.5.cloned.1.call-done), channel_id=1, replica_groups=mesh['groups'=2,'loop'=4,'enc'=2,'rep'=2] {'enc'}, dimensions={0}, use_global_device_ids=true | all-gather | bytes 589824 | tf_op jit(solution)/shard_map/all_gather | solution.py:93
  99.5 1.4 convolution_bitcast_fusion
  100.9 1.1 convolution_convert_fusion
  102.0 58.8 %all-reduce.2.cloned.1.call-done = f32[384,768]{0,1:T(8,128)} async-done(((f32[384,768]{0,1:T(8,128)}), f32[384,768]{0,1:T(8,128)}) %all-reduce.2.cloned.1.call-update) | async-done | bytes 1179664 | tf_op jit(solution)/shard_map/psum | solution.py:103
  160.8 2.7 %copy.9 = f32[384,768]{1,0:T(8,128)} copy(f32[384,768]{0,1:T(8,128)} %all-reduce.2.cloned.1.call-done) | data formatting | bytes 2359296
  (29 shorter events, 2.4 us)
Async XLA Ops:
  7.2 1.1 copy-start
  7.2 3.3 %copy-start.2 = (s32[4]{0:T(128)S(1)}, s32[4]{0:T(128)}, u32[]{:S(2)}) copy-start(s32[4]{0:T(128)} %param.9) | copy-start | bytes 52
  7.2 23.8 %reduce-scatter.3.cloned.1.call-start = ((), (), s32[]{:S(2)}) async-start(), calls=%async_computation.2 | async-start | bytes 1179648 | tf_op jit(solution)/shard_map/reduce_scatter | solution.py:30
  10.4 81.6 %reduce-scatter.5.cloned.1.call-start = ((), (), s32[]{:S(2)}) async-start(), calls=%async_computation.3 | async-start | bytes 983040 | tf_op jit(solution)/shard_map/reduce_scatter | solution.py:90
  41.5 9.0 %collective-permute-start = (bf16[128,768]{1,0:T(8,128)(2,1)S(1)}, bf16[128,768]{1,0:T(8,128)(2,1)S(1)}, u32[]{:S(2)}, u32[]{:S(2)}) collective-permute-start(bf16[128,768]{1,0:T(8,128)(2,1)S(1)} %get-tuple-element.558), channel_id=1, source_target_pairs={{0,4},{4,8},{8,12},{12,0},{1,5},{5,9},{9,13},{13,1},{2,6},{6,10},{... | collective-permute-start | bytes 589832 | tf_op jit(solution)/shard_map/while/body/eval_jaxpr/ppermute | solution.py:12
  51.7 8.2 %collective-permute-start = (bf16[128,768]{1,0:T(8,128)(2,1)S(1)}, bf16[128,768]{1,0:T(8,128)(2,1)S(1)}, u32[]{:S(2)}, u32[]{:S(2)}) collective-permute-start(bf16[128,768]{1,0:T(8,128)(2,1)S(1)} %get-tuple-element.558), channel_id=1, source_target_pairs={{0,4},{4,8},{8,12},{12,0},{1,5},{5,9},{9,13},{13,1},{2,6},{6,10},{... | collective-permute-start | bytes 589832 | tf_op jit(solution)/shard_map/while/body/eval_jaxpr/ppermute | solution.py:12
  61.1 7.5 %collective-permute-start = (bf16[128,768]{1,0:T(8,128)(2,1)S(1)}, bf16[128,768]{1,0:T(8,128)(2,1)S(1)}, u32[]{:S(2)}, u32[]{:S(2)}) collective-permute-start(bf16[128,768]{1,0:T(8,128)(2,1)S(1)} %get-tuple-element.558), channel_id=1, source_target_pairs={{0,4},{4,8},{8,12},{12,0},{1,5},{5,9},{9,13},{13,1},{2,6},{6,10},{... | collective-permute-start | bytes 589832 | tf_op jit(solution)/shard_map/while/body/eval_jaxpr/ppermute | solution.py:12
  69.8 29.7 %copy-start.1 = (bf16[256,384]{1,0:T(8,128)(2,1)S(1)}, bf16[256,384]{1,0:T(8,128)(2,1)}, u32[]{:S(2)}) copy-start(bf16[256,384]{1,0:T(8,128)(2,1)} %param.6) | copy-start | bytes 589828
  71.0 89.8 %all-reduce.2.cloned.1.call-start = ((), (), s32[]{:S(2)}) async-start(), calls=%async_computation.4 | async-start | bytes 2359296 | tf_op jit(solution)/shard_map/psum | solution.py:103
Sparse Core Ops, SparseCore 0:
  10.8 20.1 reduce-scatter.2
  71.1 20.8 reduce-scatter.4
  101.1 59.6 all-reduce.1
where the time goes:
time: 170 us
  waiting for transfers between devices  114 us (67%)
  blocking collectives  15.7 us (9%)
  between operations  13.8 us (8%)
  other arithmetic  9.37 us (6%)
  matrix products  8.66 us (5%)
  local copies, waits for them, and re-layouts  6.9 us (4%)
  starting transfers between devices  1.78 us (1%)
    psum x1, waiting for transfers between devices, body(): head_grad = lax.psum(head_part, ('loop', 'rep'))  58.8 us
    reduce_scatter x1, waiting for transfers between devices, body(): lax.psum_scatter(grad_block.astype(jnp.bfloat16), ('enc', 'rep'), scatter...  20.9 us
    ppermute x3, waiting for transfers between devices, passed_along(): return lax.ppermute(value, axis, pairs)  17 us
    reduce_scatter x1, waiting for transfers between devices, body(): lax.psum_scatter(jnp.dot(rows, head_weight, preferred_element_type=jnp.fl...  16.8 us
    all_gather x1, blocking collectives, body(): block_feats = lax.all_gather(own_feats, ('enc', 'rep'), axis=0, tiled=True)  8.2 us
    all_gather x1, blocking collectives, body(): piece = lax.all_gather(own_grad, 'enc', axis=0, tiled=True)  7.51 us
    select_n x4, other arithmetic, tile(): piece_coef = jnp.where(piece_offsets < anchor_count, piece_coef, 0.0)  5.68 us
    unnamed x7, local copies, waits for them, and re-layouts  3.67 us
  transfers between devices with their start and end apart: 6, of which 6 were waited for; matrix products, arithmetic and copies ran while one was open for 6% of the time, Pallas kernels for 0%

commit v1 on v0

--- a/solution.py
+++ b/solution.py
@@ -100,7 +100,10 @@
         rows, piece, (((0,), (0,)), ((), ())), preferred_element_type=jnp.float32
     )
     embed_part, head_part = (embed_part, head_part)
-    head_grad = lax.psum(head_part, ("loop", "rep"))
+    patches_produce = lambda page, group_axis, ax_name: lax.psum(
+        lax.psum(page, group_axis), ax_name
+    )
+    head_grad = patches_produce(head_part, "rep", ax_name="loop")
     return (embed_part.astype(jnp.bfloat16), head_grad)
 
 

time: 170 us -> 190 us (1.12)
  waiting for transfers between devices: 114 us -> 133 us
    psum x1 -> x2, waiting for transfers between devices: 58.8 us -> 78.3 us  [the longest x1 58.4 us: body(): lax.psum(lax.psum(page, group_axis), ax_name)]
  transfers between devices with their start and end apart: 6 -> 7, of which waited for: 6 -> 7; matrix products, arithmetic and copies ran while one was open for 6% -> 6% of each run, Pallas kernels for 0% -> 0%
where the time goes in v1:
time: 190 us
  waiting for transfers between devices  133 us (70%)
  blocking collectives  15.7 us (8%)
  between operations  13.8 us (7%)
  other arithmetic  9.37 us (5%)
  matrix products  8.66 us (5%)
  local copies, waits for them, and re-layouts  6.9 us (4%)
    psum x1, waiting for transfers between devices, body(): lax.psum(lax.psum(page, group_axis), ax_name)  58.4 us
    reduce_scatter x1, waiting for transfers between devices, body(): lax.psum_scatter(grad_block.astype(jnp.bfloat16), ('enc', 'rep'), scatter...  20.9 us
    psum x1, waiting for transfers between devices, body(): lax.psum(page, group_axis)  19.9 us
    ppermute x3, waiting for transfers between devices, passed_along(): return lax.ppermute(value, axis, pairs)  17 us
    reduce_scatter x1, waiting for transfers between devices, body(): lax.psum_scatter(jnp.dot(rows, head_weight, preferred_element_type=jnp.fl...  16.8 us
    all_gather x1, blocking collectives, body(): block_feats = lax.all_gather(own_feats, ('enc', 'rep'), axis=0, tiled=True)  8.2 us
    all_gather x1, blocking collectives, body(): piece = lax.all_gather(own_grad, 'enc', axis=0, tiled=True)  7.51 us
    select_n x4, other arithmetic, tile(): piece_coef = jnp.where(piece_offsets < anchor_count, piece_coef, 0.0)  5.68 us
  transfers between devices with their start and end apart: 7, of which 7 were waited for; matrix products, arithmetic and copies ran while one was open for 6% of the time, Pallas kernels for 0%

profile of v1, /device:TPU:0, one launch (start us, length us, event | category | flops | bytes accessed | tf_op | source)
XLA Modules:
  0.0 189.6 jit_solution(10322466684044067335)
XLA Ops:
  7.2 1.0 copy-done
  8.2 2.2 %fusion.40 = f32[256,768]{1,0:T(8,128)} fusion(bf16[256,384]{1,0:T(8,128)(2,1)} %param.6, bf16[384,768]{1,0:T(8,128)(2,1)S(1)} %copy-done), kind=kOutput, calls=%fused_computation.56 | convolution fusion | flops 150994944 | bytes 1572864 | tf_op jit(solution)/shard_map/dot_general | solution.py:31
  10.5 0.7 dynamic_slice.37
  11.2 0.8 dynamic_slice.39
  12.0 0.8 compare_select_fusion.1
  12.8 1.5 compare_select_fusion.2
  14.2 16.8 %reduce-scatter.3.cloned.1.call-done = f32[128,768]{1,0:T(8,128)} async-done(((f32[256,768]{1,0:T(8,128)}), f32[128,768]{1,0:T(8,128)}) %reduce-scatter.3.cloned.1.call-update) | async-done | bytes 393232 | tf_op jit(solution)/shard_map/reduce_scatter | solution.py:30
  31.0 1.1 multiply_reduce_fusion.1
  32.1 8.2 %all_gather.6 = bf16[512,768]{1,0:T(8,128)(2,1)S(1)} all-gather(bf16[128,768]{1,0:T(8,128)(2,1)S(1)} %get-tuple-element.541), channel_id=1, replica_groups=mesh['groups'=2,'loop'=4,'enc'=2,'rep'=2] {'enc','rep'}, dimensions={0}, use_global_device_ids=true | all-gather | bytes 983040 | tf_op jit(solution)/shard_map/all_gather | solution.py:36
  41.0 0.5 fusion.30
  41.5 28.3 %while.23 = (s32[]{:T(128)}, bf16[128,768]{1,0:T(8,128)(2,1)S(1)}, f32[512,768]{1,0:T(8,128)S(1)}, f32[512]{0:T(512)S(1)}, s32[]{:T(128)}, /*index=5*/s32[4]{0:T...) while((s32[]{:T(128)}, bf16[128,768]{1,0:T(8,128)(2,1)S(1)}, ...), condition=%wide.region_7.8_spmd.clone.clone, body=%wide.region_4.7_spmd.clone.clone.sunk | while | flops 203260192 | bytes 6246334 | solution.py:87
  41.5 1.5 collective-permute-start
  43.1 0.6 dynamic_slice.49
  43.6 1.4 compare_select_fusion.4
  45.1 5.5 %collective-permute-done = bf16[128,768]{1,0:T(8,128)(2,1)S(1)} collective-permute-done((bf16[128,768]{1,0:T(8,128)(2,1)S(1)}, bf16[128,768]{1,0:T(8,128)(2,1)S(1)}, u32[]{:S(2)}, u32[]{:S(2)}) %collective-permute-start) | collective-permute-done | bytes 196640 | tf_op jit(solution)/shard_map/while/body/eval_jaxpr/ppermute | solution.py:12
  51.1 0.6 convolution_add_fusion.2
  51.8 0.6 dynamic_slice.49
  52.4 1.4 compare_select_fusion.4
  53.8 6.1 %collective-permute-done = bf16[128,768]{1,0:T(8,128)(2,1)S(1)} collective-permute-done((bf16[128,768]{1,0:T(8,128)(2,1)S(1)}, bf16[128,768]{1,0:T(8,128)(2,1)S(1)}, u32[]{:S(2)}, u32[]{:S(2)}) %collective-permute-start) | collective-permute-done | bytes 196640 | tf_op jit(solution)/shard_map/while/body/eval_jaxpr/ppermute | solution.py:12
  60.5 0.6 convolution_add_fusion.2
  61.2 0.6 dynamic_slice.49
  61.8 1.4 compare_select_fusion.4
  63.2 5.4 %collective-permute-done = bf16[128,768]{1,0:T(8,128)(2,1)S(1)} collective-permute-done((bf16[128,768]{1,0:T(8,128)(2,1)S(1)}, bf16[128,768]{1,0:T(8,128)(2,1)S(1)}, u32[]{:S(2)}, u32[]{:S(2)}) %collective-permute-start) | collective-permute-done | bytes 196640 | tf_op jit(solution)/shard_map/while/body/eval_jaxpr/ppermute | solution.py:12
  69.2 0.6 convolution_add_fusion.2
  69.8 1.1 fusion.21
  71.1 20.9 %reduce-scatter.5.cloned.1.call-done = bf16[128,768]{1,0:T(8,128)(2,1)} async-done(((bf16[512,768]{1,0:T(8,128)(2,1)}), bf16[128,768]{1,0:T(8,128)(2,1)}) %reduce-scatter.5.cloned.1.call-update) | async-done | bytes 196624 | tf_op jit(solution)/shard_map/reduce_scatter | solution.py:90
  92.0 7.5 %all_gather.7 = bf16[256,768]{1,0:T(8,128)(2,1)S(1)} all-gather(bf16[128,768]{1,0:T(8,128)(2,1)} %reduce-scatter.5.cloned.1.call-done), channel_id=1, replica_groups=mesh['groups'=2,'loop'=4,'enc'=2,'rep'=2] {'enc'}, dimensions={0}, use_global_device_ids=true | all-gather | bytes 589824 | tf_op jit(solution)/shard_map/all_gather | solution.py:93
  99.5 1.4 convolution_bitcast_fusion
  101.0 19.9 %all-reduce.3.cloned.1.call-done = f32[384,768]{0,1:T(8,128)} async-done(((f32[384,768]{0,1:T(8,128)}), f32[384,768]{0,1:T(8,128)}) %all-reduce.3.cloned.1.call-update) | async-done | bytes 1179664 | tf_op jit(solution)/shard_map/psum | solution.py:104
  121.0 1.1 convolution_convert_fusion
  122.0 58.4 %all-reduce.5.cloned.1.call-done = f32[384,768]{0,1:T(8,128)} async-done(((f32[384,768]{0,1:T(8,128)}), f32[384,768]{0,1:T(8,128)}) %all-reduce.5.cloned.1.call-update) | async-done | bytes 1179664 | tf_op jit(solution)/shard_map/psum | solution.py:103
  180.4 2.7 %copy.9 = f32[384,768]{1,0:T(8,128)} copy(f32[384,768]{0,1:T(8,128)} %all-reduce.5.cloned.1.call-done) | data formatting | bytes 2359296
  (32 shorter events, 2.9 us)
Async XLA Ops:
  7.2 1.1 copy-start
  7.2 3.3 %copy-start.2 = (s32[4]{0:T(128)S(1)}, s32[4]{0:T(128)}, u32[]{:S(2)}) copy-start(s32[4]{0:T(128)} %param.9) | copy-start | bytes 52
  7.2 23.8 %reduce-scatter.3.cloned.1.call-start = ((), (), s32[]{:S(2)}) async-start(), calls=%async_computation.2 | async-start | bytes 1179648 | tf_op jit(solution)/shard_map/reduce_scatter | solution.py:30
  10.4 81.6 %reduce-scatter.5.cloned.1.call-start = ((), (), s32[]{:S(2)}) async-start(), calls=%async_computation.3 | async-start | bytes 983040 | tf_op jit(solution)/shard_map/reduce_scatter | solution.py:90
  41.5 9.0 %collective-permute-start = (bf16[128,768]{1,0:T(8,128)(2,1)S(1)}, bf16[128,768]{1,0:T(8,128)(2,1)S(1)}, u32[]{:S(2)}, u32[]{:S(2)}) collective-permute-start(bf16[128,768]{1,0:T(8,128)(2,1)S(1)} %get-tuple-element.558), channel_id=1, source_target_pairs={{0,4},{4,8},{8,12},{12,0},{1,5},{5,9},{9,13},{13,1},{2,6},{6,10},{... | collective-permute-start | bytes 589832 | tf_op jit(solution)/shard_map/while/body/eval_jaxpr/ppermute | solution.py:12
  51.7 8.2 %collective-permute-start = (bf16[128,768]{1,0:T(8,128)(2,1)S(1)}, bf16[128,768]{1,0:T(8,128)(2,1)S(1)}, u32[]{:S(2)}, u32[]{:S(2)}) collective-permute-start(bf16[128,768]{1,0:T(8,128)(2,1)S(1)} %get-tuple-element.558), channel_id=1, source_target_pairs={{0,4},{4,8},{8,12},{12,0},{1,5},{5,9},{9,13},{13,1},{2,6},{6,10},{... | collective-permute-start | bytes 589832 | tf_op jit(solution)/shard_map/while/body/eval_jaxpr/ppermute | solution.py:12
  61.1 7.5 %collective-permute-start = (bf16[128,768]{1,0:T(8,128)(2,1)S(1)}, bf16[128,768]{1,0:T(8,128)(2,1)S(1)}, u32[]{:S(2)}, u32[]{:S(2)}) collective-permute-start(bf16[128,768]{1,0:T(8,128)(2,1)S(1)} %get-tuple-element.558), channel_id=1, source_target_pairs={{0,4},{4,8},{8,12},{12,0},{1,5},{5,9},{9,13},{13,1},{2,6},{6,10},{... | collective-permute-start | bytes 589832 | tf_op jit(solution)/shard_map/while/body/eval_jaxpr/ppermute | solution.py:12
  69.8 29.7 %copy-start.1 = (bf16[256,384]{1,0:T(8,128)(2,1)S(1)}, bf16[256,384]{1,0:T(8,128)(2,1)}, u32[]{:S(2)}) copy-start(bf16[256,384]{1,0:T(8,128)(2,1)} %param.6) | copy-start | bytes 589828
  71.0 49.9 %all-reduce.3.cloned.1.call-start = ((), (), s32[]{:S(2)}) async-start(), calls=%async_computation.4 | async-start | bytes 2359296 | tf_op jit(solution)/shard_map/psum | solution.py:104
  100.9 79.5 %all-reduce.5.cloned.1.call-start = ((), (), s32[]{:S(2)}) async-start(), calls=%async_computation.5 | async-start | bytes 2359296 | tf_op jit(solution)/shard_map/psum | solution.py:103
Sparse Core Ops, SparseCore 0:
  10.8 20.1 reduce-scatter.2
  71.1 20.8 reduce-scatter.4
  101.1 19.8 all-reduce.2
  123.3 57.0 all-reduce.4
